TPU v7x, 512 devices: a whole 4x8x8 slice. The times are simulated.
512 devices in a mesh: tm: 64 (over x, y, core), space: 8 (over z).
Axes of the slice: x: 4, y: 8, z: 8, core: 2. Of those that a mesh axis runs over, the one named last changes fastest.
Arguments:
- initial: float32 [16, 128, 128], P('space'), may hold values from -6 to 6
- conductivity: float32 [16, 128, 128], P('space'), may hold values from 0.1 to 1
- source: float32 [128, 16, 128, 128], P('tm', 'space'), may hold values from -4 to 4
Outputs:
- states: float32 [128, 16, 128, 128], P('tm', 'space')
All inputs are finite; a program needn't handle non-finite values.
Results may differ from a plain program's by a relative error of at most 0.00002.
Values sent between devices are 32-bit elements; how exact they have to be, the bound alone decides.
A program may use at most 64 MiB of HBM per device.

v0:
```python
import jax
import jax.numpy as jnp
from jax import lax
from jax.sharding import PartitionSpec as P

FINE_DEV = 2
CF = 8
ITERS = 2


fine_rate = 0.02


def with_halo(cells, sides, width):
    for axis, dim in sides:
        count = lax.axis_size(axis)
        ends = count - 1
        head = lax.slice_in_dim(cells, 0, width, axis=dim)
        tail = lax.slice_in_dim(cells, cells.shape[dim] - width, cells.shape[dim], axis=dim)
        cells = jnp.concatenate(
            [
                lax.ppermute(tail, axis, [(i, (i + 1) % count) for i in range(ends)]),
                cells,
                lax.ppermute(head, axis, [((i + 1) % count, i) for i in range(ends)]),
            ],
            axis=dim,
        )
    return cells


def passed_along(value, axis, by):
    count = lax.axis_size(axis)
    pairs = [(i, i + by) for i in range(count) if 0 <= i + by < count]
    return lax.ppermute(value, axis, pairs)


def shifted(padded, step_z, step_x, step_y):
    depth, rows, cols = padded.shape
    return padded[
        1 + step_z : depth - 1 + step_z,
        1 + step_x : rows - 1 + step_x,
        1 + step_y : cols - 1 + step_y,
    ]


def diffuse(field, cond, forcing, first_plane, speed, total):
    widen = ((0, 0), (1, 1), (1, 1))
    field_pad = jnp.pad(field, widen)
    cond_pad = jnp.pad(cond, widen)
    center = shifted(field_pad, 0, 0, 0)
    kcenter = shifted(cond_pad, 0, 0, 0)
    flux = jnp.zeros_like(center)
    for offset in ((1, 0, 0), (-1, 0, 0), (0, 1, 0), (0, -1, 0), (0, 0, 1), (0, 0, -1)):
        neighbour = shifted(field_pad, offset[0], offset[1], offset[2])
        kneighbour = shifted(cond_pad, offset[0], offset[1], offset[2])
        flux = flux + 0.5 * (kcenter + kneighbour) * (neighbour - center)
    updated = center + speed * flux + forcing
    index = first_plane + 1 + jnp.arange(field.shape[0] - 2, dtype=jnp.int32)
    inside = (index >= 0) & (index < total)
    return jnp.where(inside[:, None, None], updated, jnp.float32(0.0))


def local(initial, conductivity, source):
    planes = initial.shape[0]
    rows = initial.shape[1]
    total = planes * lax.axis_size("space")
    first_plane = lax.axis_index("space") * planes
    group = CF // FINE_DEV
    share = rows // group
    position = lax.axis_index("tm") % group
    at_start = position == 0
    at_last = position == group - 1
    at_anchor = lax.axis_index("tm") == 0
    links = lax.axis_size("tm") // group - 1
    row_owner = jnp.arange(rows, dtype=jnp.int32) // share
    owned_rows = (row_owner == position)[None, :, None]
    cond_ext = with_halo(conductivity, (("space", 0),), FINE_DEV)
    cond_near = cond_ext[FINE_DEV - 1 : FINE_DEV + 1 + planes]

    def local_steps(state, pack):
        collected = []
        current = state
        for section in range(FINE_DEV):
            padded = with_halo(current, (("space", 0),), 1)
            current = diffuse(padded, cond_near, pack[section], first_plane - 1, fine_rate, total)
            collected.append(current)
        return jnp.stack(collected)

    def hand_on(field):
        return passed_along(field, "tm", 1)

    def hand_back(field):
        return passed_along(field, "tm", -1)

    def relax(start_state):
        series = local_steps(start_state, source)
        for member in range(1, group):
            current = jnp.where(at_start, start_state, hand_on(series[-1]))
            series = local_steps(current, source)
        return series

    starts = jnp.zeros_like(initial)
    for sweep in range(ITERS):
        first = relax(starts)
        relaxed = jnp.where(at_anchor, initial, hand_on(first[-1]))
        second = relax(relaxed)
        defect_full = second[-1] - first[-1]
        spread = defect_full
        for spread_hop in range(group - 1):
            spread = jnp.where(at_last, defect_full, hand_back(spread))
        defect_own = jnp.where(owned_rows, spread, jnp.float32(0.0))

        def coarse_turn(turn_index, error):
            padded = with_halo(error, (("space", 0),), 1)
            outgoing = (
                diffuse(padded, cond_near, jnp.float32(0.0), first_plane - 1, fine_rate * CF, total)
                + defect_own
            )
            return passed_along(outgoing, "tm", group)

        error = lax.fori_loop(0, links, coarse_turn, jnp.zeros_like(initial))
        summed = error
        for hop in range(group - 1):
            summed = jnp.where(at_last, error, error + hand_back(summed))
        starts = relaxed + summed
    return relax(starts)


def solution(mesh):
    return jax.shard_map(
        local,
        mesh=mesh,
        in_specs=(P("space", None, None), P("space", None, None), P("tm", "space", None, None)),
        out_specs=P("tm", "space", None, None),
        check_vma=False,
    )
```

profile of v0, /device:TPU:262, one launch (start us, length us, event | category | flops | bytes accessed | tf_op | source)
XLA Modules:
  0.0 1223.8 jit_solution(17157688835858099044)
XLA Ops:
  57.1 6.5 collective-permute-done.17
  85.0 6.5 collective-permute-done.22
  112.9 6.5 collective-permute-done.27
  140.8 6.5 collective-permute-done.32
  168.7 6.5 collective-permute-done.37
  196.6 6.5 collective-permute-done.42
  243.9 298.8 %while.24 = (s32[]{:T(128)}, f32[2,128,128]{2,1,0:T(8,128)S(1)}, s32[]{:T(128)}, f32[2,128,128]{2,1,0:T(8,128)S(1)}, f32[2,128,128]{2,1,0:T(8,128)S(1)}, /*index...) while((s32[]{:T(128)}, f32[2,128,128]{2,1,0:T(8,128)S(1)}, s32[]{:T(128)}, ...), condition=%wide.region_1.2_spmd, body=%wide.region_0.1_spmd.sunk | while | flops 2095354 | bytes 3547923 | solution.py:121
  255.6 8.9 collective-permute-done.2
  276.3 7.9 collective-permute-done.2
  296.0 7.9 collective-permute-done.2
  315.7 7.9 collective-permute-done.2
  335.3 9.0 collective-permute-done.2
  356.1 9.3 collective-permute-done.2
  377.2 8.0 collective-permute-done.2
  397.0 7.9 collective-permute-done.2
  416.7 7.9 collective-permute-done.2
  436.3 7.9 collective-permute-done.2
  456.0 7.9 collective-permute-done.2
  475.7 7.9 collective-permute-done.2
  495.4 7.9 collective-permute-done.2
  515.0 7.9 collective-permute-done.2
  534.7 7.9 collective-permute-done.2
  585.3 6.5 collective-permute-done.57
  613.2 6.5 collective-permute-done.62
  641.1 6.5 collective-permute-done.67
  669.0 6.5 collective-permute-done.72
  696.9 6.5 collective-permute-done.77
  724.7 6.5 collective-permute-done.82
  752.6 6.5 collective-permute-done.87
  799.9 298.8 %while.25 = (s32[]{:T(128)}, f32[2,128,128]{2,1,0:T(8,128)S(1)}, s32[]{:T(128)}, f32[2,128,128]{2,1,0:T(8,128)S(1)}, f32[2,128,128]{2,1,0:T(8,128)S(1)}, /*index...) while((s32[]{:T(128)}, f32[2,128,128]{2,1,0:T(8,128)S(1)}, s32[]{:T(128)}, ...), condition=%wide.region_3.4_spmd, body=%wide.region_2.3_spmd.sunk | while | flops 2095354 | bytes 3547923 | solution.py:121
  811.7 8.9 collective-permute-done.5
  832.4 7.9 collective-permute-done.5
  852.0 7.9 collective-permute-done.5
  871.7 7.9 collective-permute-done.5
  891.4 9.0 collective-permute-done.5
  912.2 9.3 collective-permute-done.5
  933.2 8.0 collective-permute-done.5
  953.0 7.9 collective-permute-done.5
  972.7 7.9 collective-permute-done.5
  992.4 7.9 collective-permute-done.5
  1012.1 7.9 collective-permute-done.5
  1031.7 7.9 collective-permute-done.5
  1051.4 7.9 collective-permute-done.5
  1071.1 7.9 collective-permute-done.5
  1090.8 7.9 collective-permute-done.5
  1141.4 6.5 collective-permute-done.102
  1169.3 6.5 collective-permute-done.107
  1197.1 6.5 collective-permute-done.112
  (637 shorter events, 871.3 us)
Async XLA Ops:
  0.0 11.7 collective-permute-start.7
  1.9 9.8 collective-permute-start.9
  27.3 8.4 collective-permute-start.12
  55.2 8.4 collective-permute-start.17
  111.0 8.4 collective-permute-start.27
  138.9 8.4 collective-permute-start.32
  194.6 8.4 collective-permute-start.42
  227.0 8.4 collective-permute-start.48
  253.7 10.9 collective-permute-start.2
  274.4 9.9 collective-permute-start.2
  294.1 9.9 collective-permute-start.2
  313.7 9.9 collective-permute-start.2
  333.4 11.0 collective-permute-start.2
  354.2 11.3 collective-permute-start.2
  375.3 10.0 collective-permute-start.2
  395.0 9.9 collective-permute-start.2
  414.7 9.9 collective-permute-start.2
  434.4 9.9 collective-permute-start.2
  454.1 9.9 collective-permute-start.2
  473.8 9.9 collective-permute-start.2
  493.4 9.9 collective-permute-start.2
  513.1 9.9 collective-permute-start.2
  532.8 9.9 collective-permute-start.2
  547.1 8.4 collective-permute-start.51
  555.5 8.4 collective-permute-start.52
  583.4 8.4 collective-permute-start.57
  639.2 8.4 collective-permute-start.67
  667.0 8.4 collective-permute-start.72
  722.8 8.4 collective-permute-start.82
  783.0 8.4 collective-permute-start.93
  791.4 8.4 collective-permute-start.94
  809.8 10.9 collective-permute-start.5
  830.4 9.9 collective-permute-start.5
  850.1 9.9 collective-permute-start.5
  869.8 9.9 collective-permute-start.5
  889.5 11.0 collective-permute-start.5
  910.2 11.3 collective-permute-start.5
  931.3 10.0 collective-permute-start.5
  951.1 9.9 collective-permute-start.5
  970.8 9.9 collective-permute-start.5
  990.4 9.9 collective-permute-start.5
  1010.1 9.9 collective-permute-start.5
  1029.8 9.9 collective-permute-start.5
  1049.5 9.9 collective-permute-start.5
  1069.2 9.9 collective-permute-start.5
  1088.8 9.9 collective-permute-start.5
  1103.1 8.4 collective-permute-start.96
  1111.6 8.4 collective-permute-start.97
  (156 other events, 1061.6 us)
where the time goes:
time: 1230 us; the launch traced here: 1220 us
  waiting for transfers between devices  627 us (51%)
  starting transfers between devices  560 us (46%)
  other arithmetic  32.1 us (3%)
    ppermute x59, waiting for transfers between devices, passed_along(): return lax.ppermute(value, axis, pairs)  385 us
    ppermute x71, starting transfers between devices, with_halo(): lax.ppermute(tail, axis, [(i, (i + 1) % count) for i in range(ends)])  278 us
    ppermute x71, waiting for transfers between devices, with_halo(): lax.ppermute(tail, axis, [(i, (i + 1) % count) for i in range(ends)])  221 us
    ppermute x59, starting transfers between devices, passed_along(): return lax.ppermute(value, axis, pairs)  145 us
    ppermute x71, starting transfers between devices, with_halo(): lax.ppermute(head, axis, [((i + 1) % count, i) for i in range(ends)])  138 us
  transfers between devices with their start and end apart: 201, of which 199 were waited for; matrix products, arithmetic and copies ran while one was open for 0% of the time, Pallas kernels for 0%

commit v1 on v0

v1 whole, which is shorter than its diff:
```python
import functools

import jax
import jax.numpy as jnp
from jax import lax
from jax.experimental import pallas as pl
from jax.experimental.pallas import tpu as pltpu
from jax.sharding import PartitionSpec as P

MESH = pl.DeviceIdType.MESH
F32 = jnp.float32
ROWS = 8
WIDE = 3 * ROWS
CHUNK = 4
LAGS = 16


def chunks(low, high):
    at = low
    while at < high:
        yield at, min(at + CHUNK, high)
        at += CHUNK


def kernel(intervals, depth, initial, cond, source, out, land_s, land_k, land_u, kx, sx, coef_a, coef_c, diag_a, diag_c,
           zed_a, zed_c, ping, pong, gsum, pair_in, v_mine, v_in, base, gam, dif, gam_w, dif_w, mixed, slots, start,
           middle, out_send, sem_s, sem_k, sem_u, sem_h, sem_p, sem_v, sem_m, sem_d, sem_o):
    tm = lax.axis_index("tm")
    z = lax.axis_index("space")
    interval = tm // 4
    quarter = tm % 4
    side = quarter // 2
    core = quarter % 2
    block = 2 * z + core
    first = interval == intervals - 1
    item = lax.rem(interval + 1, intervals)
    blocks = 2 * depth
    left = (tm - core + (1 - core), lax.rem(z + depth - (1 - core), depth))
    right = (tm - core + (1 - core), lax.rem(z + core, depth))
    pair_tm = tm - 2 * side + 2 * (1 - side)
    pair = (pair_tm, z)
    cross_tm = pair_tm - core + (1 - core)
    chip_tm = tm - core

    def interval_tm(which):
        return 4 * which + quarter

    barrier = pltpu.get_barrier_semaphore()

    def greet(device):
        pl.semaphore_signal(barrier, inc=1, device_id=device, device_id_type=MESH)

    partners = 0
    for step in range(depth):
        other = lax.rem(z + step, depth)
        greet((tm - core + (1 - core), other))
        partners += 1
        if step:
            greet((tm, other))
            partners += 1
    greet(pair)
    greet((cross_tm, left[1]))
    greet((cross_tm, right[1]))
    partners += 3
    for step in range(1, intervals):
        greet((interval_tm(lax.rem(interval + step, intervals)), z))
        partners += 1
    pl.semaphore_wait(barrier, partners)

    def send(src, dst, sems, k, device):
        pltpu.make_async_remote_copy(
            src_ref=src, dst_ref=dst, send_sem=sems.at[0, k], recv_sem=sems.at[1, k], device_id=device, device_id_type=MESH
        ).start()

    def take(ref, sems, k, way=1):
        pltpu.make_async_copy(ref, ref, sems.at[way, k]).wait()

    def spread(whole, land, sems):
        for step in range(1, depth):
            other = lax.rem(z + step, depth)
            rows = pl.ds(pl.multiple_of((2 * other + core) * ROWS, ROWS), ROWS)
            send(whole.at[:, rows], land.at[z], sems, 0, (tm, other))
        rows = pl.ds(pl.multiple_of(block * ROWS, ROWS), ROWS)
        pltpu.make_async_copy(whole.at[:, rows], land.at[z], sems.at[1, 0]).start()

    spread(cond, land_k, sem_k)
    for step in range(depth):
        other = lax.rem(z + step, depth)
        for flip in range(2):
            if step == 0 and flip == 0:
                continue
            goal = core if flip == 0 else 1 - core
            rows = pl.ds(pl.multiple_of((2 * other + goal) * ROWS, ROWS), ROWS)
            send(source.at[:, :, rows], land_s.at[core * depth + z], sem_s, 0, (chip_tm + goal, other))
    rows = pl.ds(pl.multiple_of(block * ROWS, ROWS), ROWS)
    pltpu.make_async_copy(source.at[:, :, rows], land_s.at[core * depth + z], sem_s.at[1, 0]).start()

    @pl.when(first)
    def _():
        spread(initial, land_u, sem_u)

    def gathered(land, row, parity, base_row, stride):
        flat = land.reshape(land.size // 128, 128)
        return flat[pl.ds(base_row + parity * ROWS + row, 8, stride=stride), :]

    own = pl.ds(ROWS, ROWS)

    def halo(field, sems, k, rows=ROWS):
        send(field.at[pl.ds(ROWS, rows)], field.at[pl.ds(2 * ROWS, rows)], sems, 2 * k, left)
        send(field.at[pl.ds(2 * ROWS - rows, rows)], field.at[pl.ds(ROWS - rows, rows)], sems, 2 * k + 1, right)

    def halo_take(field, sems, k, rows=ROWS, way=1):
        take(field.at[pl.ds(2 * ROWS, rows)], sems, 2 * k, way)
        take(field.at[pl.ds(ROWS - rows, rows)], sems, 2 * k + 1, way)

    take(land_k, sem_k, 0)
    for row in range(ROWS):
        for parity in range(2):
            kx[ROWS + row, parity] = gathered(land_k, row, parity, 0, 2 * ROWS)
    halo(kx, sem_h, 0)

    take(land_s, sem_s, 0)
    for pick in range(4):
        for row in range(ROWS):
            for parity in range(2):
                sx[pick, ROWS + row, parity] = gathered(
                    land_s, row, parity, (pick // 2) * depth * 4 * ROWS + (pick % 2) * 2 * ROWS, 4 * ROWS
                )
    for pick in range(4):
        halo(sx.at[pick], sem_h, 1 + pick, ROWS - 1 - pick)

    halo_take(kx, sem_h, 0)
    lane = lax.broadcasted_iota(jnp.int32, (8, 128), 1)
    sub = lax.broadcasted_iota(jnp.int32, (8, 128), 0)
    low_edge = block == 0
    high_edge = block == blocks - 1

    def kof(row, parity):
        value = kx[row, parity]
        if row < ROWS:
            value = jnp.where(low_edge, F32(0.0), value)
        if row >= 2 * ROWS:
            value = jnp.where(high_edge, F32(0.0), value)
        return value

    half = F32(0.01)
    zero = F32(0.0)
    for row in range(WIDE - 1):
        k0, k1 = kof(row, 0), kof(row, 1)
        za = half * (k0 + k1)
        zb_all = half * (k1 + jnp.where(sub == 7, zero, pltpu.roll(k0, 7, 0)))
        zb_off = jnp.where(sub == 7, zero, zb_all)
        zc_all = half * (k0 + jnp.where(sub == 0, zero, pltpu.roll(k1, 1, 0)))
        zc_off = jnp.where(sub == 0, zero, zc_all)
        zed_a[row, 0], zed_a[row, 1], zed_a[row, 2] = za, zc_off, zb_off
        zed_c[row, 0], zed_c[row, 1], zed_c[row, 2] = 8.0 * za, 8.0 * zc_off, 8.0 * zb_off
        for parity, here in enumerate((k0, k1)):
            up_all = half * (here + kof(row + 1, parity))
            up_off = up_all
            if row == ROWS - 1:
                up_off = jnp.where(low_edge, zero, up_all)
            if row == 2 * ROWS - 1:
                up_off = jnp.where(high_edge, zero, up_all)
            yp_all = half * (here + jnp.where(lane == 127, zero, pltpu.roll(here, 127, 1)))
            yp_off = jnp.where(lane == 127, zero, yp_all)
            ym_all = half * (here + jnp.where(lane == 0, zero, pltpu.roll(here, 1, 1)))
            ym_off = jnp.where(lane == 0, zero, ym_all)
            coef_a[0, row, parity], coef_c[0, row, parity] = up_off, 8.0 * up_off
            if row:
                down_all = half * (here + kof(row - 1, parity))
                total = (za + (zc_all if parity == 0 else zb_all)) + (yp_all + ym_all) + (up_all + down_all)
                coef_a[1, row, parity], coef_c[1, row, parity] = yp_off, 8.0 * yp_off
                coef_a[2, row, parity], coef_c[2, row, parity] = ym_off, 8.0 * ym_off
                diag_a[row, parity], diag_c[row, parity] = 1.0 - total, 1.0 - 8.0 * total

    fine = (coef_a, diag_a, zed_a)
    coarse = (coef_c, diag_c, zed_c)

    def stencil(ops, src, a, b):
        coef, diag, zed = ops
        n = b - a
        here = [src[pl.ds(a, n), parity] for parity in range(2)]
        outs = []
        for parity in range(2):
            u = here[parity]
            across = here[1 - parity]
            turned = pltpu.roll(across, 1 if parity == 0 else 7, 1)
            vert = zed[pl.ds(a, n), 0] * across + zed[pl.ds(a, n), 1 + parity] * turned
            rows = coef[0, pl.ds(a, n), parity] * src[pl.ds(a + 1, n), parity] \
                + coef[0, pl.ds(a - 1, n), parity] * src[pl.ds(a - 1, n), parity]
            cols = coef[1, pl.ds(a, n), parity] * pltpu.roll(u, 127, 2) + coef[2, pl.ds(a, n), parity] * pltpu.roll(u, 1, 2)
            outs.append((diag[pl.ds(a, n), parity] * u + rows) + (vert + cols))
        return outs

    def apply(ops, src, dst, low, high, forcing=None):
        for a, b in chunks(low, high):
            outs = stencil(ops, src, a, b)
            for parity in range(2):
                value = outs[parity]
                if forcing is not None:
                    value = value + forcing[pl.ds(a, b - a), parity]
                dst[pl.ds(a, b - a), parity] = value

    def run(ops, src, dst, steps, reach, spare):
        current = src
        for step in range(steps):
            reach -= 1
            goal = dst if step == steps - 1 else spare[step % 2]
            apply(ops, current, goal, ROWS - reach, 2 * ROWS + reach)
            current = goal

    spare = (ping, pong)

    for pick in range(4):
        halo_take(sx.at[pick], sem_h, 1 + pick, ROWS - 1 - pick)
    apply(fine, sx.at[0], ping, 2, 22, sx.at[1])
    apply(fine, ping, pong, 3, 21, sx.at[2])
    apply(fine, pong, v_mine, 4, 20, sx.at[3])
    run(fine, v_mine, gsum, 4, 4, spare)

    @pl.when(side == 1)
    def _():
        gsum[own] = v_mine[own]

    send(gsum.at[own], pair_in, sem_p, 0, pair)

    @pl.when(side == 0)
    def _():
        send(v_mine.at[pl.ds(4, 16)], v_in.at[pl.ds(4, 16)], sem_v, 0, pair)

    take(pair_in, sem_p, 0)

    @pl.when(first)
    def _():
        take(land_u, sem_u, 0)
        for row in range(ROWS):
            for parity in range(2):
                base[0, ROWS + row, parity] = gathered(land_u, row, parity, 0, 2 * ROWS)

    @pl.when(jnp.logical_not(first))
    def _():
        base[0, own] = gsum[own] + pair_in[...]

    mine = pl.ds(ROWS + 4 * side, 4)

    def post(n, src):
        @pl.when(item + n < intervals)
        def _():
            send(src, slots.at[n], sem_m, n, (interval_tm(item + n), z))

    for power in range(3):
        halo(base.at[power], sem_h, 5 + power)
        post(power, base.at[power, mine])
        halo_take(base.at[power], sem_h, 5 + power)
        if power < 2:
            run(fine, base.at[power], base.at[power + 1], 8, 8, spare)
    apply(coarse, base.at[2], dif.at[0], ROWS, 2 * ROWS)
    run(fine, base.at[2], gam.at[0], 8, 8, spare)
    dif[0, own] = gam[0, own] - dif[0, own]

    for turn in range(13):
        at, inner = turn // 8, turn % 8
        if inner == 0:
            now_g, now_d = gam.at[at], dif.at[at]
            wide = 8 if at == 0 else 4
            halo(now_g, sem_h, 8 + 2 * at, wide)
            halo(now_d, sem_h, 9 + 2 * at, wide)
        if turn == 0:
            post(3, now_g.at[mine])
        else:
            mixed[turn] = now_g[mine] + F32(turn) * now_d[mine]
            if turn < 12:
                post(3 + turn, mixed.at[turn])
        if inner == 0:
            halo_take(now_g, sem_h, 8 + 2 * at, wide)
            halo_take(now_d, sem_h, 9 + 2 * at, wide)
            reach = wide
        if turn == 12:
            break
        reach -= 1
        last = inner == 7
        next_g = gam.at[at + 1] if last else gam_w.at[inner % 2]
        next_d = dif.at[at + 1] if last else dif_w.at[inner % 2]
        apply(coarse, now_g, next_g, ROWS - reach, 2 * ROWS + reach)
        apply(coarse, now_d, next_d, ROWS - reach, 2 * ROWS + reach)
        now_g, now_d = next_g, next_d

    start[mine] = jnp.where(first, mixed[12], jnp.zeros_like(mixed[12]))
    for n in range(LAGS - 1):
        @pl.when(n <= interval)
        def _():
            take(slots.at[n], sem_m, n)
            start[mine] = start[mine] + slots[n]

    below = pl.ds(4 * side, 4)
    above = pl.ds(2 * ROWS + 4 * side, 4)
    send(start.at[mine], start.at[mine], sem_d, 0, pair)
    send(start.at[mine], start.at[above], sem_d, 1, left)
    send(start.at[mine], start.at[below], sem_d, 2, right)
    send(start.at[mine], start.at[above], sem_d, 3, (cross_tm, left[1]))
    send(start.at[mine], start.at[below], sem_d, 4, (cross_tm, right[1]))
    for k in range(5):
        take(slots.at[0], sem_d, k)

    run(fine, start, middle, 4, 8, spare)

    @pl.when(side == 0)
    def _():
        middle[pl.ds(4, 16)] = start[pl.ds(4, 16)]

    @pl.when(side == 1)
    def _():
        take(v_in.at[pl.ds(4, 16)], sem_v, 0)
        middle[pl.ds(4, 16)] = middle[pl.ds(4, 16)] + v_in[pl.ds(4, 16)]

    flat = out_send.reshape(out_send.size // 128, 128)
    current = middle
    my_rows = pl.ds(pl.multiple_of(block * ROWS, ROWS), ROWS)
    for pick in range(4):
        goal = spare[pick % 2]
        reach = 3 - pick
        apply(fine, current, goal, ROWS - reach, 2 * ROWS + reach, sx.at[pick])
        current = goal
        origin = (pick // 2) * depth * 4 * ROWS + (pick % 2) * 2 * ROWS
        for row in range(ROWS):
            for parity in range(2):
                flat[pl.ds(origin + parity * ROWS + row, 8, stride=4 * ROWS), :] = goal[ROWS + row, parity]
        if pick % 2:
            goal_core = pick // 2
            for step in range(1, depth):
                other = lax.rem(z + step, depth)
                send(out_send.at[goal_core, other], out.at[:, :, my_rows], sem_o, 0, (chip_tm + goal_core, other))

            @pl.when(core == goal_core)
            def _():
                pltpu.make_async_copy(out_send.at[goal_core, z], out.at[:, :, my_rows], sem_o.at[1, 0]).start()

            @pl.when(core != goal_core)
            def _():
                send(out_send.at[goal_core, z], out.at[:, :, my_rows], sem_o, 0, (chip_tm + goal_core, z))

    take(out, sem_o, 0)

    take(land_k.at[pl.ds(0, depth - 1)], sem_k, 0, 0)
    take(land_s.at[pl.ds(0, 2 * depth - 1)], sem_s, 0, 0)

    @pl.when(first)
    def _():
        take(land_u.at[pl.ds(0, depth - 1)], sem_u, 0, 0)

    @pl.when(side == 0)
    def _():
        take(v_in.at[pl.ds(4, 16)], sem_v, 0, 0)

    halo_take(kx, sem_h, 0, ROWS, 0)
    for pick in range(4):
        halo_take(sx.at[pick], sem_h, 1 + pick, ROWS - 1 - pick, 0)
    take(pair_in, sem_p, 0, 0)
    for power in range(3):
        halo_take(base.at[power], sem_h, 5 + power, ROWS, 0)
    for at, wide in ((0, 8), (1, 4)):
        halo_take(gam.at[at], sem_h, 8 + 2 * at, wide, 0)
        halo_take(dif.at[at], sem_h, 9 + 2 * at, wide, 0)
    for n in range(LAGS - 1):
        @pl.when(item + n < intervals)
        def _():
            take(slots.at[n], sem_m, n, 0)
    for k in range(5):
        take(slots.at[0], sem_d, k, 0)
    take(land_s.at[pl.ds(0, 2 * depth - 1)], sem_o, 0, 0)


def local(intervals, depth, initial, cond, source):
    def vm(*shape):
        return pltpu.VMEM(shape, F32)

    def field(*lead):
        return vm(*lead, WIDE, 2, 8, 128)

    dma = pltpu.SemaphoreType.DMA
    return pl.pallas_call(
        functools.partial(kernel, intervals, depth),
        out_shape=jax.ShapeDtypeStruct(source.shape, F32),
        in_specs=[pl.BlockSpec(memory_space=pl.ANY)] * 3,
        out_specs=pl.BlockSpec(memory_space=pl.ANY),
        scratch_shapes=[
            vm(2 * depth, 2, 2, ROWS, 128),
            vm(depth, 2, ROWS, 128),
            vm(depth, 2, ROWS, 128),
            field(),
            field(4),
            field(3),
            field(3),
            field(),
            field(),
            vm(WIDE, 3, 8, 128),
            vm(WIDE, 3, 8, 128),
            field(),
            field(),
            field(),
            vm(ROWS, 2, 8, 128),
            field(),
            field(),
            field(3),
            field(2),
            field(2),
            field(2),
            field(2),
            vm(13, 4, 2, 8, 128),
            vm(LAGS, 4, 2, 8, 128),
            field(),
            field(),
            vm(2, depth, 2, 2, ROWS, 128),
            dma((2, 1)),
            dma((2, 1)),
            dma((2, 1)),
            dma((2, 24)),
            dma((2, 1)),
            dma((2, 1)),
            dma((2, LAGS)),
            dma((2, 5)),
            dma((2, 1)),
        ],
        compiler_params=pltpu.CompilerParams(
            collective_id=0, has_side_effects=True, vmem_limit_bytes=40 * 1024 * 1024
        ),
        name="mgrit",
    )(initial, cond, source)


def solution(mesh):
    intervals = mesh.shape["tm"] // 4
    depth = mesh.shape["space"]
    return jax.shard_map(
        functools.partial(local, intervals, depth),
        mesh=mesh,
        in_specs=(P("space", None, None), P("space", None, None), P("tm", "space", None, None)),
        out_specs=P("tm", "space", None, None),
        check_vma=False,
    )
```

time: 1230 us -> 77.1 us (0.06)
  the two profiles are of different devices: /device:TPU:262 before, /device:TPU:63 now
where the time goes in v1:
time: 77.1 us; the launch traced here: 76.9 us
  Pallas kernels  73.5 us (95%)
  local copies, waits for them, and re-layouts  3.46 us (4%)
    pallas_call x1, Pallas kernels, local(): pl.pallas_call(functools.partial(kernel, intervals, depth), out_shape=jax...  73.5 us
    unnamed x7, local copies, waits for them, and re-layouts  3.46 us

profile of v1, /device:TPU:63, one launch (start us, length us, event | category | flops | bytes accessed | tf_op | source)
XLA Modules:
  0.0 76.9 jit_solution(18359215607706727367)
XLA Ops:
  0.0 0.0 copy-start
  0.0 0.9 %copy-done = f32[2,2,128,128]{3,2,1,0:T(8,128)S(1)} copy-done((f32[2,2,128,128]{3,2,1,0:T(8,128)S(1)}, f32[2,2,128,128]{3,2,1,0:T(8,128)}, u32[]{:S(2)}) %copy-start) | copy-done | bytes 262168
  1.0 0.0 copy-start.1
  1.0 0.9 %copy-done.1 = f32[2,128,128]{2,1,0:T(8,128)S(1)} copy-done((f32[2,128,128]{2,1,0:T(8,128)S(1)}, f32[2,128,128]{2,1,0:T(8,128)}, u32[]{:S(2)}) %copy-start.1) | copy-done | bytes 131096
  1.9 0.0 copy-start.2
  1.9 0.9 %copy-done.2 = f32[2,128,128]{2,1,0:T(8,128)S(1)} copy-done((f32[2,128,128]{2,1,0:T(8,128)S(1)}, f32[2,128,128]{2,1,0:T(8,128)}, u32[]{:S(2)}) %copy-start.2) | copy-done | bytes 131096
  2.8 73.5 %mgrit.1 = f32[2,2,128,128]{3,2,1,0:T(8,128)S(1)} custom-call(f32[2,128,128]{2,1,0:T(8,128)S(1)} %copy-done.1, f32[2,128,128]{2,1,0:T(8,128)S(1)} %copy-done.2, f32[2,2,128,128]{3,2,1,0:T(8,128)S(1)} %copy-done), custom_call_target="tpu_custom_call" | custom-call | tf_op jit(solution)/shard_map/mgrit/pallas_call | solution.py:381
  76.2 0.7 copy.5
Async XLA Ops:
  0.0 0.9 %copy-start = (f32[2,2,128,128]{3,2,1,0:T(8,128)S(1)}, f32[2,2,128,128]{3,2,1,0:T(8,128)}, u32[]{:S(2)}) copy-start(f32[2,2,128,128]{3,2,1,0:T(8,128)} %source.1) | copy-start | bytes 786436
  1.0 0.9 %copy-start.1 = (f32[2,128,128]{2,1,0:T(8,128)S(1)}, f32[2,128,128]{2,1,0:T(8,128)}, u32[]{:S(2)}) copy-start(f32[2,128,128]{2,1,0:T(8,128)} %initial.1) | copy-start | bytes 393220
  1.9 0.9 %copy-start.2 = (f32[2,128,128]{2,1,0:T(8,128)S(1)}, f32[2,128,128]{2,1,0:T(8,128)}, u32[]{:S(2)}) copy-start(f32[2,128,128]{2,1,0:T(8,128)} %cond.1) | copy-start | bytes 393220

commit v2 on v1

--- a/solution.py
+++ b/solution.py
@@ -10,7 +10,8 @@
 MESH = pl.DeviceIdType.MESH
 F32 = jnp.float32
 ROWS = 8
-WIDE = 3 * ROWS
+OWN = 2 * ROWS
+WIDE = 5 * ROWS
 CHUNK = 4
 LAGS = 16
 
@@ -103,33 +104,43 @@
         flat = land.reshape(land.size // 128, 128)
         return flat[pl.ds(base_row + parity * ROWS + row, 8, stride=stride), :]
 
-    own = pl.ds(ROWS, ROWS)
-
-    def halo(field, sems, k, rows=ROWS):
-        send(field.at[pl.ds(ROWS, rows)], field.at[pl.ds(2 * ROWS, rows)], sems, 2 * k, left)
-        send(field.at[pl.ds(2 * ROWS - rows, rows)], field.at[pl.ds(ROWS - rows, rows)], sems, 2 * k + 1, right)
-
-    def halo_take(field, sems, k, rows=ROWS, way=1):
-        take(field.at[pl.ds(2 * ROWS, rows)], sems, 2 * k, way)
-        take(field.at[pl.ds(ROWS - rows, rows)], sems, 2 * k + 1, way)
+    own = pl.ds(OWN, ROWS)
+    left2 = (tm, lax.rem(z + depth - 1, depth))
+    right2 = (tm, lax.rem(z + 1, depth))
+
+    def halo(field, k, rows):
+        send(field.at[pl.ds(OWN, rows)], field.at[pl.ds(OWN + ROWS, rows)], sem_h, k, left)
+        send(field.at[pl.ds(OWN + ROWS - rows, rows)], field.at[pl.ds(OWN - rows, rows)], sem_h, k + 1, right)
+
+    def halo_take(field, k, rows, way=1):
+        take(field.at[pl.ds(OWN + ROWS, rows)], sem_h, k, way)
+        take(field.at[pl.ds(OWN - rows, rows)], sem_h, k + 1, way)
+
+    def wide_halo(field, k):
+        for turn, (device, at) in enumerate(((left, 3), (right, 1), (left2, 4), (right2, 0))):
+            send(field.at[own], field.at[pl.ds(at * ROWS, ROWS)], sem_h, k + turn, device)
+
+    def wide_take(field, k, way=1):
+        for turn, at in enumerate((3, 1, 4, 0)):
+            take(field.at[pl.ds(at * ROWS, ROWS)], sem_h, k + turn, way)
 
     take(land_k, sem_k, 0)
     for row in range(ROWS):
         for parity in range(2):
-            kx[ROWS + row, parity] = gathered(land_k, row, parity, 0, 2 * ROWS)
-    halo(kx, sem_h, 0)
+            kx[OWN + row, parity] = gathered(land_k, row, parity, 0, 2 * ROWS)
+    wide_halo(kx, 0)
 
     take(land_s, sem_s, 0)
     for pick in range(4):
         for row in range(ROWS):
             for parity in range(2):
-                sx[pick, ROWS + row, parity] = gathered(
+                sx[pick, OWN + row, parity] = gathered(
                     land_s, row, parity, (pick // 2) * depth * 4 * ROWS + (pick % 2) * 2 * ROWS, 4 * ROWS
                 )
     for pick in range(4):
-        halo(sx.at[pick], sem_h, 1 + pick, ROWS - 1 - pick)
-
-    halo_take(kx, sem_h, 0)
+        halo(sx.at[pick], 4 + 2 * pick, ROWS - 1 - pick)
+
+    wide_take(kx, 0)
     lane = lax.broadcasted_iota(jnp.int32, (8, 128), 1)
     sub = lax.broadcasted_iota(jnp.int32, (8, 128), 0)
     low_edge = block == 0
@@ -137,10 +148,10 @@
 
     def kof(row, parity):
         value = kx[row, parity]
-        if row < ROWS:
-            value = jnp.where(low_edge, F32(0.0), value)
-        if row >= 2 * ROWS:
-            value = jnp.where(high_edge, F32(0.0), value)
+        if row < OWN:
+            value = jnp.where(low_edge if row >= ROWS else block <= 1, F32(0.0), value)
+        if row >= OWN + ROWS:
+            value = jnp.where(high_edge if row < OWN + 2 * ROWS else block >= blocks - 2, F32(0.0), value)
         return value
 
     half = F32(0.01)
@@ -157,10 +168,9 @@
         for parity, here in enumerate((k0, k1)):
             up_all = half * (here + kof(row + 1, parity))
             up_off = up_all
-            if row == ROWS - 1:
-                up_off = jnp.where(low_edge, zero, up_all)
-            if row == 2 * ROWS - 1:
-                up_off = jnp.where(high_edge, zero, up_all)
+            for edge, at in ((block == 1, 1), (low_edge, 2), (high_edge, 3), (block == blocks - 2, 4)):
+                if row == at * ROWS - 1:
+                    up_off = jnp.where(edge, zero, up_all)
             yp_all = half * (here + jnp.where(lane == 127, zero, pltpu.roll(here, 127, 1)))
             yp_off = jnp.where(lane == 127, zero, yp_all)
             ym_all = half * (here + jnp.where(lane == 0, zero, pltpu.roll(here, 1, 1)))
@@ -206,83 +216,85 @@
         for step in range(steps):
             reach -= 1
             goal = dst if step == steps - 1 else spare[step % 2]
-            apply(ops, current, goal, ROWS - reach, 2 * ROWS + reach)
+            apply(ops, current, goal, OWN - reach, OWN + ROWS + reach)
             current = goal
 
     spare = (ping, pong)
 
     for pick in range(4):
-        halo_take(sx.at[pick], sem_h, 1 + pick, ROWS - 1 - pick)
-    apply(fine, sx.at[0], ping, 2, 22, sx.at[1])
-    apply(fine, ping, pong, 3, 21, sx.at[2])
-    apply(fine, pong, v_mine, 4, 20, sx.at[3])
+        halo_take(sx.at[pick], 4 + 2 * pick, ROWS - 1 - pick)
+    apply(fine, sx.at[0], ping, OWN - 6, OWN + ROWS + 6, sx.at[1])
+    apply(fine, ping, pong, OWN - 5, OWN + ROWS + 5, sx.at[2])
+    apply(fine, pong, v_mine, OWN - 4, OWN + ROWS + 4, sx.at[3])
     run(fine, v_mine, gsum, 4, 4, spare)
 
     @pl.when(side == 1)
     def _():
         gsum[own] = v_mine[own]
-
-    send(gsum.at[own], pair_in, sem_p, 0, pair)
-
-    @pl.when(side == 0)
-    def _():
-        send(v_mine.at[pl.ds(4, 16)], v_in.at[pl.ds(4, 16)], sem_v, 0, pair)
-
-    take(pair_in, sem_p, 0)
 
     @pl.when(first)
     def _():
         take(land_u, sem_u, 0)
         for row in range(ROWS):
             for parity in range(2):
-                base[0, ROWS + row, parity] = gathered(land_u, row, parity, 0, 2 * ROWS)
-
-    @pl.when(jnp.logical_not(first))
-    def _():
-        base[0, own] = gsum[own] + pair_in[...]
-
-    mine = pl.ds(ROWS + 4 * side, 4)
+                gsum[OWN + row, parity] = jnp.where(side == 0, gathered(land_u, row, parity, 0, 2 * ROWS), zero)
+
+    send(gsum.at[own], pair_in.at[own], sem_p, 0, pair)
+    take(pair_in.at[own], sem_p, 0)
+    base[0, own] = gsum[own] + pair_in[own]
+    wide_halo(base.at[0], 12)
+
+    mine = pl.ds(OWN + 4 * side, 4)
 
     def post(n, src):
         @pl.when(item + n < intervals)
         def _():
             send(src, slots.at[n], sem_m, n, (interval_tm(item + n), z))
 
-    for power in range(3):
-        halo(base.at[power], sem_h, 5 + power)
-        post(power, base.at[power, mine])
-        halo_take(base.at[power], sem_h, 5 + power)
-        if power < 2:
-            run(fine, base.at[power], base.at[power + 1], 8, 8, spare)
-    apply(coarse, base.at[2], dif.at[0], ROWS, 2 * ROWS)
-    run(fine, base.at[2], gam.at[0], 8, 8, spare)
-    dif[0, own] = gam[0, own] - dif[0, own]
+    post(0, base.at[0, mine])
+    wide_take(base.at[0], 12)
+    run(fine, base.at[0], base.at[1], 8, 16, spare)
+    post(1, base.at[1, mine])
+    run(fine, base.at[1], base.at[2], 8, 8, spare)
+    wide_halo(base.at[2], 16)
+    post(2, base.at[2, mine])
+
+    @pl.when(side == 0)
+    def _():
+        send(v_mine.at[pl.ds(OWN - 4, 16)], v_in.at[pl.ds(OWN - 4, 16)], sem_v, 0, pair)
+
+    wide_take(base.at[2], 16)
+    apply(coarse, base.at[2], dif.at[0], OWN - ROWS, OWN + 2 * ROWS)
+    run(fine, base.at[2], gam.at[0], 8, 16, spare)
+    inner_rows = pl.ds(OWN - ROWS, 3 * ROWS)
+    dif[0, inner_rows] = gam[0, inner_rows] - dif[0, inner_rows]
 
     for turn in range(13):
         at, inner = turn // 8, turn % 8
         if inner == 0:
             now_g, now_d = gam.at[at], dif.at[at]
-            wide = 8 if at == 0 else 4
-            halo(now_g, sem_h, 8 + 2 * at, wide)
-            halo(now_d, sem_h, 9 + 2 * at, wide)
+            reach = 8
+            if at:
+                reach = 4
+                halo(now_g, 20, reach)
+                halo(now_d, 22, reach)
         if turn == 0:
             post(3, now_g.at[mine])
         else:
             mixed[turn] = now_g[mine] + F32(turn) * now_d[mine]
             if turn < 12:
                 post(3 + turn, mixed.at[turn])
-        if inner == 0:
-            halo_take(now_g, sem_h, 8 + 2 * at, wide)
-            halo_take(now_d, sem_h, 9 + 2 * at, wide)
-            reach = wide
+        if inner == 0 and at:
+            halo_take(now_g, 20, reach)
+            halo_take(now_d, 22, reach)
         if turn == 12:
             break
         reach -= 1
         last = inner == 7
         next_g = gam.at[at + 1] if last else gam_w.at[inner % 2]
         next_d = dif.at[at + 1] if last else dif_w.at[inner % 2]
-        apply(coarse, now_g, next_g, ROWS - reach, 2 * ROWS + reach)
-        apply(coarse, now_d, next_d, ROWS - reach, 2 * ROWS + reach)
+        apply(coarse, now_g, next_g, OWN - reach, OWN + ROWS + reach)
+        apply(coarse, now_d, next_d, OWN - reach, OWN + ROWS + reach)
         now_g, now_d = next_g, next_d
 
     start[mine] = jnp.where(first, mixed[12], jnp.zeros_like(mixed[12]))
@@ -292,8 +304,8 @@
             take(slots.at[n], sem_m, n)
             start[mine] = start[mine] + slots[n]
 
-    below = pl.ds(4 * side, 4)
-    above = pl.ds(2 * ROWS + 4 * side, 4)
+    below = pl.ds(OWN - ROWS + 4 * side, 4)
+    above = pl.ds(OWN + ROWS + 4 * side, 4)
     send(start.at[mine], start.at[mine], sem_d, 0, pair)
     send(start.at[mine], start.at[above], sem_d, 1, left)
     send(start.at[mine], start.at[below], sem_d, 2, right)
@@ -306,12 +318,12 @@
 
     @pl.when(side == 0)
     def _():
-        middle[pl.ds(4, 16)] = start[pl.ds(4, 16)]
+        middle[pl.ds(OWN - 4, 16)] = start[pl.ds(OWN - 4, 16)]
 
     @pl.when(side == 1)
     def _():
-        take(v_in.at[pl.ds(4, 16)], sem_v, 0)
-        middle[pl.ds(4, 16)] = middle[pl.ds(4, 16)] + v_in[pl.ds(4, 16)]
+        take(v_in.at[pl.ds(OWN - 4, 16)], sem_v, 0)
+        middle[pl.ds(OWN - 4, 16)] = middle[pl.ds(OWN - 4, 16)] + v_in[pl.ds(OWN - 4, 16)]
 
     flat = out_send.reshape(out_send.size // 128, 128)
     current = middle
@@ -319,12 +331,12 @@
     for pick in range(4):
         goal = spare[pick % 2]
         reach = 3 - pick
-        apply(fine, current, goal, ROWS - reach, 2 * ROWS + reach, sx.at[pick])
+        apply(fine, current, goal, OWN - reach, OWN + ROWS + reach, sx.at[pick])
         current = goal
         origin = (pick // 2) * depth * 4 * ROWS + (pick % 2) * 2 * ROWS
         for row in range(ROWS):
             for parity in range(2):
-                flat[pl.ds(origin + parity * ROWS + row, 8, stride=4 * ROWS), :] = goal[ROWS + row, parity]
+                flat[pl.ds(origin + parity * ROWS + row, 8, stride=4 * ROWS), :] = goal[OWN + row, parity]
         if pick % 2:
             goal_core = pick // 2
             for step in range(1, depth):
@@ -339,8 +351,6 @@
             def _():
                 send(out_send.at[goal_core, z], out.at[:, :, my_rows], sem_o, 0, (chip_tm + goal_core, z))
 
-    take(out, sem_o, 0)
-
     take(land_k.at[pl.ds(0, depth - 1)], sem_k, 0, 0)
     take(land_s.at[pl.ds(0, 2 * depth - 1)], sem_s, 0, 0)
 
@@ -350,17 +360,16 @@
 
     @pl.when(side == 0)
     def _():
-        take(v_in.at[pl.ds(4, 16)], sem_v, 0, 0)
-
-    halo_take(kx, sem_h, 0, ROWS, 0)
+        take(v_in.at[pl.ds(OWN - 4, 16)], sem_v, 0, 0)
+
+    wide_take(kx, 0, 0)
     for pick in range(4):
-        halo_take(sx.at[pick], sem_h, 1 + pick, ROWS - 1 - pick, 0)
-    take(pair_in, sem_p, 0, 0)
-    for power in range(3):
-        halo_take(base.at[power], sem_h, 5 + power, ROWS, 0)
-    for at, wide in ((0, 8), (1, 4)):
-        halo_take(gam.at[at], sem_h, 8 + 2 * at, wide, 0)
-        halo_take(dif.at[at], sem_h, 9 + 2 * at, wide, 0)
+        halo_take(sx.at[pick], 4 + 2 * pick, ROWS - 1 - pick, 0)
+    take(gsum.at[own], sem_p, 0, 0)
+    wide_take(base.at[0], 12, 0)
+    wide_take(base.at[2], 16, 0)
+    halo_take(gam.at[1], 20, 4, 0)
+    halo_take(dif.at[1], 22, 4, 0)
     for n in range(LAGS - 1):
         @pl.when(item + n < intervals)
         def _():
@@ -368,6 +377,7 @@
     for k in range(5):
         take(slots.at[0], sem_d, k, 0)
     take(land_s.at[pl.ds(0, 2 * depth - 1)], sem_o, 0, 0)
+    take(out, sem_o, 0)
 
 
 def local(intervals, depth, initial, cond, source):
@@ -398,7 +408,7 @@
             field(),
             field(),
             field(),
-            vm(ROWS, 2, 8, 128),
+            field(),
             field(),
             field(),
             field(3),
@@ -415,14 +425,14 @@
             dma((2, 1)),
             dma((2, 1)),
             dma((2, 24)),
-            dma((2, 1)),
+            dma((2, 5)),
             dma((2, 1)),
             dma((2, LAGS)),
             dma((2, 5)),
             dma((2, 1)),
         ],
         compiler_params=pltpu.CompilerParams(
-            collective_id=0, has_side_effects=True, vmem_limit_bytes=40 * 1024 * 1024
+            collective_id=0, has_side_effects=True, vmem_limit_bytes=60 * 1024 * 1024
         ),
         name="mgrit",
     )(initial, cond, source)

time: 77.1 us -> 71.3 us (0.925)
  Pallas kernels: 73.5 us -> 69.5 us
  local copies, waits for them, and re-layouts: 3.46 us -> 1.67 us
    pallas_call x1, Pallas kernels: 73.5 us -> 69.5 us  [local(): pl.pallas_call(functools.partial(kernel, intervals, depth), out_shape=jax...]
    unnamed x7 -> x1, local copies, waits for them, and re-layouts: 3.46 us -> 1.67 us
where the time goes in v2:
time: 71.3 us; the launch traced here: 71.2 us
  Pallas kernels  69.5 us (97%)
  local copies, waits for them, and re-layouts  1.67 us (2%)
    pallas_call x1, Pallas kernels, local(): pl.pallas_call(functools.partial(kernel, intervals, depth), out_shape=jax...  69.5 us
    unnamed x1, local copies, waits for them, and re-layouts  1.67 us

profile of v2, /device:TPU:63, one launch (start us, length us, event | category | flops | bytes accessed | tf_op | source)
XLA Modules:
  0.0 71.2 jit_solution(6190810716617802812)
XLA Ops:
  0.0 69.5 %mgrit.1 = f32[2,2,128,128]{3,2,1,0:T(8,128)} custom-call(f32[2,128,128]{2,1,0:T(8,128)} %initial.1, f32[2,128,128]{2,1,0:T(8,128)} %cond.1, f32[2,2,128,128]{3,2,1,0:T(8,128)} %source.1), custom_call_target="tpu_custom_call" | custom-call | tf_op jit(solution)/shard_map/mgrit/pallas_call | solution.py:391
  69.5 1.7 %copy.5 = f32[2,2,128,128]{3,2,1,0:T(8,128)} copy(f32[2,2,128,128]{3,2,1,0:T(8,128)} %mgrit.1) | data formatting | bytes 524288

commit v3 on v2

--- a/solution.py
+++ b/solution.py
@@ -23,9 +23,9 @@
         at += CHUNK
 
 
-def kernel(intervals, depth, initial, cond, source, out, land_s, land_k, land_u, kx, sx, coef_a, coef_c, diag_a, diag_c,
+def kernel(intervals, depth, far_initial, far_cond, far_source, out, initial, cond, source, land_s, land_k, land_u, kx, sx, coef_a, coef_c, diag_a, diag_c,
            zed_a, zed_c, ping, pong, gsum, pair_in, v_mine, v_in, base, gam, dif, gam_w, dif_w, mixed, slots, start,
-           middle, out_send, sem_s, sem_k, sem_u, sem_h, sem_p, sem_v, sem_m, sem_d, sem_o):
+           middle, out_send, sem_s, sem_k, sem_u, sem_h, sem_p, sem_v, sem_m, sem_d, sem_o, sem_i):
     tm = lax.axis_index("tm")
     z = lax.axis_index("space")
     interval = tm // 4
@@ -46,6 +46,13 @@
     def interval_tm(which):
         return 4 * which + quarter
 
+    fetches = [
+        pltpu.make_async_copy(there, here, sem_i.at[k])
+        for k, (there, here) in enumerate(((far_cond, cond), (far_source, source), (far_initial, initial)))
+    ]
+    for fetch in fetches:
+        fetch.start()
+
     barrier = pltpu.get_barrier_semaphore()
 
     def greet(device):
@@ -66,6 +73,8 @@
     for step in range(1, intervals):
         greet((interval_tm(lax.rem(interval + step, intervals)), z))
         partners += 1
+    for fetch in fetches:
+        fetch.wait()
     pl.semaphore_wait(barrier, partners)
 
     def send(src, dst, sems, k, device):
@@ -128,7 +137,7 @@
     for row in range(ROWS):
         for parity in range(2):
             kx[OWN + row, parity] = gathered(land_k, row, parity, 0, 2 * ROWS)
-    wide_halo(kx, 0)
+    halo(kx, 0, ROWS)
 
     take(land_s, sem_s, 0)
     for pick in range(4):
@@ -139,8 +148,10 @@
                 )
     for pick in range(4):
         halo(sx.at[pick], 4 + 2 * pick, ROWS - 1 - pick)
-
-    wide_take(kx, 0)
+    send(kx.at[own], kx.at[pl.ds(4 * ROWS, ROWS)], sem_h, 2, left2)
+    send(kx.at[own], kx.at[pl.ds(0, ROWS)], sem_h, 3, right2)
+
+    halo_take(kx, 0, ROWS)
     lane = lax.broadcasted_iota(jnp.int32, (8, 128), 1)
     sub = lax.broadcasted_iota(jnp.int32, (8, 128), 0)
     low_edge = block == 0
@@ -156,7 +167,7 @@
 
     half = F32(0.01)
     zero = F32(0.0)
-    for row in range(WIDE - 1):
+    def coefficients(row, below):
         k0, k1 = kof(row, 0), kof(row, 1)
         za = half * (k0 + k1)
         zb_all = half * (k1 + jnp.where(sub == 7, zero, pltpu.roll(k0, 7, 0)))
@@ -176,12 +187,15 @@
             ym_all = half * (here + jnp.where(lane == 0, zero, pltpu.roll(here, 1, 1)))
             ym_off = jnp.where(lane == 0, zero, ym_all)
             coef_a[0, row, parity], coef_c[0, row, parity] = up_off, 8.0 * up_off
-            if row:
+            if below:
                 down_all = half * (here + kof(row - 1, parity))
                 total = (za + (zc_all if parity == 0 else zb_all)) + (yp_all + ym_all) + (up_all + down_all)
                 coef_a[1, row, parity], coef_c[1, row, parity] = yp_off, 8.0 * yp_off
                 coef_a[2, row, parity], coef_c[2, row, parity] = ym_off, 8.0 * ym_off
                 diag_a[row, parity], diag_c[row, parity] = 1.0 - total, 1.0 - 8.0 * total
+
+    for row in range(ROWS, 4 * ROWS - 1):
+        coefficients(row, row > ROWS)
 
     fine = (coef_a, diag_a, zed_a)
     coarse = (coef_c, diag_c, zed_c)
@@ -240,6 +254,10 @@
                 gsum[OWN + row, parity] = jnp.where(side == 0, gathered(land_u, row, parity, 0, 2 * ROWS), zero)
 
     send(gsum.at[own], pair_in.at[own], sem_p, 0, pair)
+    take(kx.at[pl.ds(4 * ROWS, ROWS)], sem_h, 2)
+    take(kx.at[pl.ds(0, ROWS)], sem_h, 3)
+    for row in (*range(ROWS + 1), *range(4 * ROWS - 1, WIDE - 1)):
+        coefficients(row, row > 0)
     take(pair_in.at[own], sem_p, 0)
     base[0, own] = gsum[own] + pair_in[own]
     wide_halo(base.at[0], 12)
@@ -339,7 +357,7 @@
                 flat[pl.ds(origin + parity * ROWS + row, 8, stride=4 * ROWS), :] = goal[OWN + row, parity]
         if pick % 2:
             goal_core = pick // 2
-            for step in range(1, depth):
+            for step in (4, 3, 5, 2, 6, 1, 7):
                 other = lax.rem(z + step, depth)
                 send(out_send.at[goal_core, other], out.at[:, :, my_rows], sem_o, 0, (chip_tm + goal_core, other))
 
@@ -394,6 +412,9 @@
         in_specs=[pl.BlockSpec(memory_space=pl.ANY)] * 3,
         out_specs=pl.BlockSpec(memory_space=pl.ANY),
         scratch_shapes=[
+            vm(*initial.shape),
+            vm(*cond.shape),
+            vm(*source.shape),
             vm(2 * depth, 2, 2, ROWS, 128),
             vm(depth, 2, ROWS, 128),
             vm(depth, 2, ROWS, 128),
@@ -430,6 +451,7 @@
             dma((2, LAGS)),
             dma((2, 5)),
             dma((2, 1)),
+            dma((3,)),
         ],
         compiler_params=pltpu.CompilerParams(
             collective_id=0, has_side_effects=True, vmem_limit_bytes=60 * 1024 * 1024

time: 71.3 us -> 70.7 us (level)
  no operation moved by 1% of the time
where the time goes in v3:
time: 70.7 us; the launch traced here: 70.6 us
  Pallas kernels  68.9 us (97%)
  local copies, waits for them, and re-layouts  1.67 us (2%)
    pallas_call x1, Pallas kernels, local(): pl.pallas_call(functools.partial(kernel, intervals, depth), out_shape=jax...  68.9 us
    unnamed x1, local copies, waits for them, and re-layouts  1.67 us

profile of v3, /device:TPU:63, one launch (start us, length us, event | category | flops | bytes accessed | tf_op | source)
XLA Modules:
  0.0 70.6 jit_solution(6831028869098017390)
XLA Ops:
  0.0 68.9 %mgrit.1 = f32[2,2,128,128]{3,2,1,0:T(8,128)} custom-call(f32[2,128,128]{2,1,0:T(8,128)} %far_initial.1, f32[2,128,128]{2,1,0:T(8,128)} %far_cond.1, f32[2,2,128,128]{3,2,1,0:T(8,128)} %far_source.1), custom_call_target="tpu_custom_call" | custom-call | tf_op jit(solution)/shard_map/mgrit/pallas_call | solution.py:409
  68.9 1.7 %copy.5 = f32[2,2,128,128]{3,2,1,0:T(8,128)} copy(f32[2,2,128,128]{3,2,1,0:T(8,128)} %mgrit.1) | data formatting | bytes 524288

commit v4 on v3

--- a/solution.py
+++ b/solution.py
@@ -50,16 +50,13 @@
         pltpu.make_async_copy(there, here, sem_i.at[k])
         for k, (there, here) in enumerate(((far_cond, cond), (far_source, source), (far_initial, initial)))
     ]
-    for fetch in fetches:
-        fetch.start()
-
     barrier = pltpu.get_barrier_semaphore()
 
     def greet(device):
         pl.semaphore_signal(barrier, inc=1, device_id=device, device_id_type=MESH)
 
     partners = 0
-    for step in range(depth):
+    for step in sorted(range(depth), key=lambda at: -min(at, depth - at)):
         other = lax.rem(z + step, depth)
         greet((tm - core + (1 - core), other))
         partners += 1
@@ -73,6 +70,8 @@
     for step in range(1, intervals):
         greet((interval_tm(lax.rem(interval + step, intervals)), z))
         partners += 1
+    for fetch in fetches:
+        fetch.start()
     for fetch in fetches:
         fetch.wait()
     pl.semaphore_wait(barrier, partners)
@@ -235,10 +234,12 @@
 
     spare = (ping, pong)
 
-    for pick in range(4):
+    for pick in range(2):
         halo_take(sx.at[pick], 4 + 2 * pick, ROWS - 1 - pick)
     apply(fine, sx.at[0], ping, OWN - 6, OWN + ROWS + 6, sx.at[1])
+    halo_take(sx.at[2], 8, ROWS - 3)
     apply(fine, ping, pong, OWN - 5, OWN + ROWS + 5, sx.at[2])
+    halo_take(sx.at[3], 10, ROWS - 4)
     apply(fine, pong, v_mine, OWN - 4, OWN + ROWS + 4, sx.at[3])
     run(fine, v_mine, gsum, 4, 4, spare)
 
@@ -294,7 +295,6 @@
             reach = 8
             if at:
                 reach = 4
-                halo(now_g, 20, reach)
                 halo(now_d, 22, reach)
         if turn == 0:
             post(3, now_g.at[mine])
@@ -312,6 +312,8 @@
         next_g = gam.at[at + 1] if last else gam_w.at[inner % 2]
         next_d = dif.at[at + 1] if last else dif_w.at[inner % 2]
         apply(coarse, now_g, next_g, OWN - reach, OWN + ROWS + reach)
+        if last:
+            halo(next_g, 20, 4)
         apply(coarse, now_d, next_d, OWN - reach, OWN + ROWS + reach)
         now_g, now_d = next_g, next_d
 

time: 70.7 us -> 70.7 us (level)
  no operation moved by 1% of the time
where the time goes in v4:
time: 70.7 us; the launch traced here: 70.6 us
  Pallas kernels  68.9 us (97%)
  local copies, waits for them, and re-layouts  1.67 us (2%)
    pallas_call x1, Pallas kernels, local(): pl.pallas_call(functools.partial(kernel, intervals, depth), out_shape=jax...  68.9 us
    unnamed x1, local copies, waits for them, and re-layouts  1.67 us

profile of v4, /device:TPU:63, one launch (start us, length us, event | category | flops | bytes accessed | tf_op | source)
XLA Modules:
  0.0 70.6 jit_solution(823201915346063390)
XLA Ops:
  0.0 68.9 %mgrit.1 = f32[2,2,128,128]{3,2,1,0:T(8,128)} custom-call(f32[2,128,128]{2,1,0:T(8,128)} %far_initial.1, f32[2,128,128]{2,1,0:T(8,128)} %far_cond.1, f32[2,2,128,128]{3,2,1,0:T(8,128)} %far_source.1), custom_call_target="tpu_custom_call" | custom-call | tf_op jit(solution)/shard_map/mgrit/pallas_call | solution.py:411
  68.9 1.7 %copy.5 = f32[2,2,128,128]{3,2,1,0:T(8,128)} copy(f32[2,2,128,128]{3,2,1,0:T(8,128)} %mgrit.1) | data formatting | bytes 524288
